TPU v7x, 32 devices: a whole 2x2x4 slice. The times are simulated.
32 devices in a mesh: tm: 16 (over z, y, x), rows: 2 (over core).
Axes of the slice: x: 2, y: 2, z: 4, core: 2. Of those that a mesh axis runs over, the one named last changes fastest.
Arguments:
- snapshots: bfloat16 [128, 32, 2048], P('tm', 'rows'), may hold values from -8 to 8
- tile_masks: int32 [128, 4, 16], P('tm', 'rows'), may hold values from 0 to 1, as said below
- widths: int32 [128, 2], P('tm'), may hold values from 1 to 4
Outputs:
- excess_map: float32 [2, 32, 2048], P(None, 'rows', 'tm')
- peak_map: float32 [2, 32, 2048], P(None, 'rows')
Inputs may be any that keep to these rules, and one draw needn't show every extreme that they name: `tile_masks`: 1 keeps the 8 x 128 tile of a snapshot, 0 rejects it.
All inputs are finite; a program needn't handle non-finite values.
Results may differ from a plain program's by a relative error of at most 0.0036.
Values may be sent and summed in bfloat16 or wider, within the bound.
A program may use at most 64 MiB of HBM per device.

v0:
```python
import jax
import jax.numpy as jnp
from jax import lax
from jax.sharding import PartitionSpec as P

HISTORY_FRAMES = 64
RADIUS = 8
TILE_R = 8
TILE_C = 128


threshold = 0.5


def padded(value, sides, width):
    for axis, dim in sides:
        count, length = (lax.axis_size(axis), value.shape[dim])
        up = [(i, (i + 1) % count) for i in range(count - 1)]
        down = [(j, i) for i, j in up]
        last = lax.slice_in_dim(value, length - width, length, axis=dim)
        first = lax.slice_in_dim(value, 0, width, axis=dim)
        before = lax.ppermute(last, axis, up)
        after = lax.ppermute(first, axis, down)
        value = jnp.concatenate([before, value, after], axis=dim)
    return value


def filter_taps(widths):
    sigma_val = widths.astype(jnp.float32)[..., None]
    offsets = jnp.arange(-RADIUS, RADIUS + 1).astype(jnp.float32)
    weights = jnp.exp(-(offsets * offsets) / (2.0 * sigma_val * sigma_val))
    return (weights / jnp.sqrt(jnp.sum(weights * weights, axis=-1, keepdims=True))).astype(
        jnp.bfloat16
    )


def history_band(local_times, back_step):
    target = jnp.arange(local_times)[:, None]
    source = jnp.arange(local_times)[None, :]
    distance = back_step * local_times + target - source
    return ((distance >= 1) & (distance <= HISTORY_FRAMES)).astype(jnp.bfloat16)


def tap_onehot(target_count):
    taps_count = 2 * RADIUS + 1
    source = jnp.arange(target_count + 2 * RADIUS)[:, None, None]
    target = jnp.arange(target_count)[None, :, None]
    return (source - target == jnp.arange(taps_count)[None, None, :]).astype(jnp.float32)


def column_residual(snapshots, tile_masks, widths):
    moved = lax.all_to_all(snapshots, "tm", split_axis=2, concat_axis=0, tiled=True)
    all_masks, all_widths = (
        lax.all_gather(tile_masks, "tm", axis=0, tiled=True),
        lax.all_gather(widths, "tm", axis=0, tiled=True),
    )
    total_times, local_rows, own_cols = moved.shape
    patch_rows = all_masks.shape[1]
    first_col = lax.axis_index("tm") * own_cols
    tile_of = (first_col + jnp.arange(own_cols)) // TILE_C
    pick = (jnp.arange(all_masks.shape[2])[:, None] == tile_of[None, :]).astype(jnp.float32)
    keep_tiles = jnp.einsum("trk,kc->trc", all_masks.astype(jnp.float32), pick)
    keep_pixels = jnp.broadcast_to(
        keep_tiles[:, :, None, :], (total_times, patch_rows, TILE_R, own_cols)
    ).reshape(total_times, local_rows, own_cols)
    pixels = local_rows * own_cols
    keep_flat = keep_pixels.astype(jnp.bfloat16).reshape(total_times, pixels)
    masked = moved.reshape(total_times, pixels) * keep_flat
    block_count = total_times // HISTORY_FRAMES
    own_band = history_band(HISTORY_FRAMES, 0)
    back_band = history_band(HISTORY_FRAMES, 1)
    empty_block = jnp.zeros((1, HISTORY_FRAMES, pixels), jnp.bfloat16)
    value_blocks = masked.reshape(block_count, HISTORY_FRAMES, pixels)
    keep_blocks = keep_flat.reshape(block_count, HISTORY_FRAMES, pixels)
    value_prior = jnp.concatenate([empty_block, value_blocks[:-1]], axis=0)
    keep_prior = jnp.concatenate([empty_block, keep_blocks[:-1]], axis=0)
    window = jnp.einsum("js,bsp->bjp", own_band, value_blocks, preferred_element_type=jnp.float32)
    window = window + jnp.einsum(
        "js,bsp->bjp", back_band, value_prior, preferred_element_type=jnp.float32
    )
    counts = jnp.einsum("js,bsp->bjp", own_band, keep_blocks, preferred_element_type=jnp.float32)
    counts = counts + jnp.einsum(
        "js,bsp->bjp", back_band, keep_prior, preferred_element_type=jnp.float32
    )
    mean_img = (window / jnp.maximum(counts, 1.0)).reshape(total_times, local_rows, own_cols)
    residual = (keep_pixels * (moved.astype(jnp.float32) - mean_img)).astype(jnp.bfloat16)
    return (residual, filter_taps(all_widths).astype(jnp.float32))


def body(snapshots, tile_masks, widths):
    residual, kernel = column_residual(snapshots, tile_masks, widths)
    local_times, local_rows, column_count = residual.shape
    padded_rows = padded(residual, (("rows", 1),), RADIUS)
    row_onehot = tap_onehot(local_rows)
    row_results = []
    for filter_index in range(widths.shape[1]):
        row_weights = jnp.einsum(
            "jik,tk->tij", row_onehot, kernel[:, filter_index], precision=lax.Precision.HIGHEST
        ).astype(jnp.bfloat16)
        row_results.append(
            jnp.einsum(
                "tij,tjc->tic", row_weights, padded_rows, preferred_element_type=jnp.float32
            ).astype(jnp.bfloat16)
        )
    stacked_rows = jnp.stack(row_results)
    padded_cols = padded(stacked_rows, (("tm", 3),), RADIUS)
    column_onehot = tap_onehot(column_count)
    excess_terms = []
    peak_terms = []
    for filter_index in range(widths.shape[1]):
        column_weights = jnp.einsum(
            "jck,tk->tjc", column_onehot, kernel[:, filter_index], precision=lax.Precision.HIGHEST
        ).astype(jnp.bfloat16)
        filtered = jnp.einsum(
            "trj,tjc->trc",
            padded_cols[filter_index],
            column_weights,
            preferred_element_type=jnp.float32,
        )
        excess_terms.append(jnp.sum(jnp.maximum(filtered - threshold, 0.0), axis=0))
        peak_terms.append(jnp.max(filtered, axis=0))
    excess_map = jnp.stack(excess_terms) / local_times
    peak_map = lax.all_gather(jnp.stack(peak_terms), "tm", axis=2, tiled=True)
    return (excess_map, peak_map)


def solution(mesh):
    return jax.shard_map(
        body,
        mesh=mesh,
        in_specs=(P("tm", "rows", None), P("tm", "rows", None), P("tm", None)),
        out_specs=(P(None, "rows", "tm"), P(None, "rows", None)),
        check_vma=False,
    )
```

profile of v0, /device:TPU:0, one launch (start us, length us, event | category | flops | bytes accessed | tf_op | source)
XLA Modules:
  0.0 190.9 jit_solution(9750065384838639887)
XLA Ops:
  0.6 5.3 %copy.35 = bf16[8,16,2048]{1,0,2:T(8,128)(2,1)} copy(bf16[8,16,2048]{2,1,0:T(8,128)(2,1)} %param.3) | data formatting | bytes 1048576 | tf_op args[0]
  6.0 6.4 %reshape.110 = bf16[16,2,8192]{2,1,0:T(2,128)(2,1)} reshape(bf16[2048,8,16]{2,1,0:T(8,128)(2,1)} %bitcast.84) | data formatting | bytes 1048576
  12.4 8.4 %all-to-all-start = ((bf16[16,2,8192]{2,1,0:T(2,128)(2,1)}), bf16[16,2,8192]{2,1,0:T(2,128)(2,1)S(1)}, u32[]{:S(2)}, u32[]{:S(2)}) async-start(bf16[16,2,8192]{2,1,0:T(2,128)(2,1)} %reshape.110), calls=%async_computation | async-start | bytes 1048576 | tf_op jit(solution)/shard_map/all_to_all | solution.py:52
  20.9 0.0 copy-done.4
  20.9 43.1 %all_gather.10 = s32[128,2,16]{2,1,0:T(2,128)S(1)} all-gather(s32[8,2,16]{2,1,0:T(2,128)S(1)} %copy-done.4), channel_id=1, replica_groups=mesh['tm'=16,'rows'=2] {'tm'}, dimensions={0}, use_global_device_ids=true | all-gather | bytes 17408 | tf_op jit(solution)/shard_map/all_gather | solution.py:54
  63.9 0.1 copy.33
  64.0 0.2 fusion.59
  64.3 0.1 copy.34
  64.4 0.1 broadcast_bitcast_fusion
  64.5 37.4 %all-gather = s32[16,8,2]{1,2,0:T(2,128)S(1)} all-gather(s32[1,8,2]{1,2,0:T(2,128)S(1)} %bitcast.96), channel_id=1, replica_groups=mesh['tm'=16,'rows'=2] {'tm'}, dimensions={0}, use_global_device_ids=true | all-gather | bytes 1088 | tf_op jit(solution)/shard_map/all_gather | solution.py:55
  101.8 0.1 copy.31
  101.9 0.1 copy.32
  102.0 0.1 reshape.104
  102.1 0.1 multiply_reduce_fusion
  102.2 0.1 divide_convert_fusion
  102.3 0.1 copy.38
  102.4 0.1 broadcast_in_dim.5
  102.5 0.2 convert_element_type.75
  102.8 0.1 copy.58
  102.9 0.1 slice.42
  103.1 0.2 convolution_convert_fusion.5
  103.3 1.2 copy.39
  104.5 0.2 convolution_convert_fusion.4
  104.8 1.2 copy.40
  106.0 1.3 fusion.27
  107.2 0.0 all-to-all-done
  107.2 4.1 %reshape.111 = bf16[2048,8,16]{2,1,0:T(8,128)(2,1)} reshape(bf16[16,2,8192]{2,1,0:T(2,128)(2,1)S(1)} %all-to-all-done) | data formatting | bytes 1048576
  111.4 4.4 %copy.36 = bf16[8,16,16,128]{3,0,1,2:T(8,128)(2,1)S(1)} copy(bf16[8,16,16,128]{1,0,3,2:T(8,128)(2,1)} %bitcast.83) | data formatting | bytes 1048576 | tf_op jit(solution)/shard_map/all_to_all | solution.py:52
  115.8 0.1 bitcast_convert_fusion
  115.9 0.3 fusion.12
  116.2 0.4 convolution_add_fusion.1
  116.6 0.6 copy-done.1
  117.1 0.4 fusion.5
  117.5 0.2 copy.48
  117.7 0.2 copy.37
  117.9 0.3 fusion.9
  118.2 1.3 collective-permute-start
  119.5 0.0 copy-start.2
  119.6 1.4 collective-permute-start.1
  121.0 3.5 %convolution_convert_fusion.1 = bf16[128,144,128]{2,0,1:T(8,128)(2,1)} fusion(s32[144,128]{1,0:T(8,128)S(1)} %iota_subtract_fusion, bf16[128,2,17]{0,2,1:T(8,128)(2,1)S(1)} %divide_convert_fusion), kind=kOutput, calls=%fused_computation.5 | convolution fusion | flops 82888704 | bytes 4798464 | tf_op jit(solution)/shard_map/jck,tk->tjc/dot_general | solution.py:111
  124.5 0.0 collective-permute-done
  124.5 0.0 collective-permute-done.1
  124.5 0.4 fusion.6
  125.0 0.6 copy-done.3
  125.6 0.4 fusion.7
  126.0 0.0 copy-start
  126.0 0.5 slice_maximum_fusion
  126.5 0.8 copy.41
  127.3 2.1 %collective-permute-start.2 = (bf16[2,128,16,8]{1,3,2,0:T(8,128)(2,1)S(1)}, bf16[2,128,16,8]{1,3,2,0:T(8,128)(2,1)S(1)}, u32[]{:S(2)}, u32[]{:S(2)}) collective-permute-start(bf16[2,128,16,8]{1,3,2,0:T(8,128)(2,1)S(1)} %copy.41), channel_id=1, source_target_pairs={{0,2},{2,4},{4,6},{6,8},{8,10},{10,12},{12,14},{14,16},{16,18},{18... | collective-permute-start | bytes 196616 | tf_op jit(solution)/shard_map/ppermute | solution.py:22
  129.4 0.8 copy.42
  130.2 1.5 collective-permute-start.3
  131.7 3.6 %convolution_convert_fusion = bf16[128,144,128]{2,0,1:T(8,128)(2,1)} fusion(s32[144,128]{1,0:T(8,128)S(1)} %iota_subtract_fusion, bf16[128,2,17]{0,2,1:T(8,128)(2,1)S(1)} %divide_convert_fusion), kind=kOutput, calls=%fused_computation.4 | convolution fusion | flops 82888704 | bytes 4798464 | tf_op jit(solution)/shard_map/jck,tk->tjc/dot_general | solution.py:111
  135.2 0.0 collective-permute-done.2
  135.2 0.8 copy.43
  136.0 0.9 collective-permute-done.3
  136.9 0.8 copy.44
  137.7 0.0 slice-start.1
  137.7 2.4 %pad_maximum_fusion = bf16[2,128,16,144]{3,2,1,0:T(8,128)(2,1)S(1)} fusion(bf16[2,128,16,8]{3,2,1,0:T(8,128)(2,1)S(1)} %copy.44, bf16[1,128,16,128]{3,2,1,0:T(8,128)(2,1)} %copy-done, bf16[1,128,16,128]{3,2,1,0:T(8,128)(2,1)S(1)} %fusion.6, bf16[2,128,16,8]{3,2,1,0:T(8,128)(2,1)S(1)} %copy.43), kind=kLoop, calls=%fused_computation.10 | loop fusion | flops 4718592 | bytes 2359296 | tf_op jit(solution)/shard_map/concatenate | solution.py:24
  140.1 6.6 %fusion.56 = (f32[16,128]{1,0:T(8,128)S(1)}, f32[16,128]{1,0:T(8,128)S(1)}) fusion(bf16[128,144,128]{2,0,1:T(8,128)(2,1)} %convolution_convert_fusion.1, bf16[2,128,16,144]{3,2,1,0:T(8,128)(2,1)S(1)} %pad_maximum_fusion), kind=kOutput, calls=%fused_computation.94 | convolution fusion | flops 76541952 | bytes 5783552 | tf_op jit(solution)/shard_map/trj,tjc->trc/dot_general | solution.py:114
  146.7 0.0 slice-done.1
  146.7 4.3 %fusion.57 = (f32[16,128]{1,0:T(8,128)S(1)}, f32[16,128]{1,0:T(8,128)S(1)}) fusion(bf16[128,144,128]{2,0,1:T(8,128)(2,1)S(1)} %bitcast.88, bf16[2,128,16,144]{3,2,1,0:T(8,128)(2,1)S(1)} %pad_maximum_fusion), kind=kOutput, calls=%fused_computation.95 | convolution fusion | flops 76541952 | bytes 5783552 | tf_op jit(solution)/shard_map/trj,tjc->trc/dot_general | solution.py:114
  151.0 38.6 %all_gather.11 = f32[2,16,2048]{2,1,0:T(8,128)S(1)} all-gather(f32[2,16,128]{2,1,0:T(8,128)S(1)} %pad_maximum_fusion.5), channel_id=1, replica_groups=mesh['tm'=16,'rows'=2] {'tm'}, dimensions={2}, use_global_device_ids=true | all-gather | bytes 278528 | tf_op jit(solution)/shard_map/all_gather | solution.py:123
  189.6 0.6 maximum_multiply_fusion
  190.2 0.7 copy.60
  (21 shorter events, 0.1 us)
Async XLA Ops:
  6.0 14.9 %copy-start.4 = (s32[8,2,16]{2,1,0:T(2,128)S(1)}, s32[8,2,16]{2,1,0:T(2,128)}, u32[]{:S(2)}) copy-start(s32[8,2,16]{2,1,0:T(2,128)} %param.4) | copy-start | bytes 3076
  12.4 52.1 %copy-start.5 = (s32[8,2]{0,1:T(2,128)S(1)}, s32[8,2]{0,1:T(2,128)}, u32[]{:S(2)}) copy-start(s32[8,2]{0,1:T(2,128)} %param.5) | copy-start | bytes 196
  12.4 94.8 %all-to-all-start = ((bf16[16,2,8192]{2,1,0:T(2,128)(2,1)}), bf16[16,2,8192]{2,1,0:T(2,128)(2,1)S(1)}, u32[]{:S(2)}, u32[]{:S(2)}) async-start(bf16[16,2,8192]{2,1,0:T(2,128)(2,1)} %reshape.110), calls=%async_computation | async-start | bytes 1048576 | tf_op jit(solution)/shard_map/all_to_all | solution.py:52
  115.9 1.2 copy-start.1
  118.2 6.3 %collective-permute-start = (bf16[128,8,128]{2,1,0:T(8,128)(2,1)S(1)}, bf16[128,8,128]{2,1,0:T(8,128)(2,1)S(1)}, u32[]{:S(2)}, u32[]{:S(2)}) collective-permute-start(bf16[128,8,128]{2,1,0:T(8,128)(2,1)S(1)} %get-tuple-element.8), channel_id=1, source_target_pairs={{0,1},{2,3},{4,5},{6,7},{8,9},{10,11},{12,13},{14,15},{16,17},{18,... | collective-permute-start | bytes 786440 | tf_op jit(solution)/shard_map/ppermute | solution.py:22
  119.5 5.0 %copy-start.2 = (bf16[128,32,16]{1,2,0:T(8,128)(2,1)S(1)}, bf16[128,32,16]{1,2,0:T(8,128)(2,1)}, u32[]{:S(2)}) copy-start(bf16[128,32,16]{1,2,0:T(8,128)(2,1)} %copy.39) | copy-start | bytes 393220
  119.6 5.0 %collective-permute-start.1 = (bf16[128,8,128]{2,1,0:T(8,128)(2,1)S(1)}, bf16[128,8,128]{2,1,0:T(8,128)(2,1)S(1)}, u32[]{:S(2)}, u32[]{:S(2)}) collective-permute-start(bf16[128,8,128]{2,1,0:T(8,128)(2,1)S(1)} %get-tuple-element.9), channel_id=1, source_target_pairs={{1,0},{3,2},{5,4},{7,6},{9,8},{11,10},{13,12},{15,14},{17,16},{19,... | collective-permute-start | bytes 786440 | tf_op jit(solution)/shard_map/ppermute | solution.py:23
  124.5 1.0 copy-start.3
  126.0 10.0 %copy-start = (bf16[1,128,16,128]{3,2,1,0:T(8,128)(2,1)}, bf16[1,128,16,128]{3,2,1,0:T(8,128)(2,1)S(1)}, u32[]{:S(2)}) copy-start(bf16[1,128,16,128]{3,2,1,0:T(8,128)(2,1)S(1)} %fusion.7) | copy-start | bytes 1572868
  127.3 8.0 %collective-permute-start.2 = (bf16[2,128,16,8]{1,3,2,0:T(8,128)(2,1)S(1)}, bf16[2,128,16,8]{1,3,2,0:T(8,128)(2,1)S(1)}, u32[]{:S(2)}, u32[]{:S(2)}) collective-permute-start(bf16[2,128,16,8]{1,3,2,0:T(8,128)(2,1)S(1)} %copy.41), channel_id=1, source_target_pairs={{0,2},{2,4},{4,6},{6,8},{8,10},{10,12},{12,14},{14,16},{16,18},{18... | collective-permute-start | bytes 196616 | tf_op jit(solution)/shard_map/ppermute | solution.py:22
  130.2 6.7 %collective-permute-start.3 = (bf16[2,128,16,8]{1,3,2,0:T(8,128)(2,1)S(1)}, bf16[2,128,16,8]{1,3,2,0:T(8,128)(2,1)S(1)}, u32[]{:S(2)}, u32[]{:S(2)}) collective-permute-start(bf16[2,128,16,8]{1,3,2,0:T(8,128)(2,1)S(1)} %copy.42), channel_id=1, source_target_pairs={{2,0},{4,2},{6,4},{8,6},{10,8},{12,10},{14,12},{16,14},{18,16},{20... | collective-permute-start | bytes 196616 | tf_op jit(solution)/shard_map/ppermute | solution.py:23
  135.2 11.4 %slice-start = ((s8[4718592]{0:T(1024)(128)(4,1)}), s8[524288]{0:T(1024)(128)(4,1)S(1)}, s32[]{:S(2)}) async-start(s8[4718592]{0:T(1024)(128)(4,1)} %bitcast.87), calls=%async_computation.1 | async-start | bytes 1048576
  137.7 9.0 %slice-start.1 = ((s8[4718592]{0:T(1024)(128)(4,1)}), s8[4194304]{0:T(1024)(128)(4,1)S(1)}, s32[]{:S(2)}) async-start(s8[4718592]{0:T(1024)(128)(4,1)} %bitcast.87), calls=%async_computation.2 | async-start | bytes 8388608
where the time goes:
time: 192 us; the launch traced here: 191 us
  blocking collectives  119 us (62%)
  local copies, waits for them, and re-layouts  29.4 us (15%)
  matrix products  21.9 us (11%)
  starting transfers between devices  14.7 us (8%)
  other arithmetic  4.06 us (2%)
    all_gather x1, blocking collectives, column_residual(): lax.all_gather(tile_masks, 'tm', axis=0, tiled=True)  43.1 us
    all_gather x1, blocking collectives, body(): peak_map = lax.all_gather(jnp.stack(peak_terms), 'tm', axis=2, tiled=True)  38.6 us
    all_gather x1, blocking collectives, column_residual(): lax.all_gather(widths, 'tm', axis=0, tiled=True)  37.4 us
    unnamed x22, local copies, waits for them, and re-layouts  18.1 us
    dot_general x2, matrix products, body(): jnp.einsum('trj,tjc->trc', padded_cols[filter_index], column_weights, pre...  10.9 us
    all_to_all x1, starting transfers between devices, column_residual(): lax.all_to_all(snapshots, 'tm', split_axis=2, concat_axis=0, tiled=True)  8.44 us
    dot_general x2, matrix products, body(): jnp.einsum('jck,tk->tjc', column_onehot, kernel[:, filter_index], precisi...  7.14 us
    all_to_all x1, local copies, waits for them, and re-layouts, column_residual(): lax.all_to_all(snapshots, 'tm', split_axis=2, concat_axis=0, tiled=True)  4.41 us
  transfers between devices with their start and end apart: 5, of which 1 were waited for; matrix products, arithmetic and copies ran while one was open for 8% of the time, Pallas kernels for 0%

commit v1 on v0

--- a/solution.py
+++ b/solution.py
@@ -1,6 +1,11 @@
+import functools
+import math
+
 import jax
 import jax.numpy as jnp
 from jax import lax
+from jax.experimental import pallas as pl
+from jax.experimental.pallas import tpu as pltpu
 from jax.sharding import PartitionSpec as P
 
 HISTORY_FRAMES = 64
@@ -124,9 +129,402 @@
     return (excess_map, peak_map)
 
 
+MESH = pl.DeviceIdType.MESH
+WIDTHS = 4
+LANES = 128
+HALO_ROWS = 8
+
+
+def tap_values(offset, width):
+    norm = math.sqrt(sum(math.exp(-(k * k) / (width * width)) for k in range(-RADIUS, RADIUS + 1)))
+    value = jnp.exp(offset * offset * (-1.0 / (2.0 * width * width))) / norm
+    return jnp.where(jnp.abs(offset) <= RADIUS, value, 0.0)
+
+
+def pick_width(width, options):
+    first, second, third, fourth = options
+    return jnp.where(
+        width == 1.0,
+        first,
+        jnp.where(width == 2.0, second, jnp.where(width == 3.0, third, fourth)),
+    )
+
+
+def search_kernel(
+    n,
+    x_ref,
+    meta_ref,
+    exc_ref,
+    peak_ref,
+    x_all,
+    halo_out,
+    halo_all,
+    meta_all,
+    keep_rows,
+    scale_rows,
+    width_rows,
+    masked,
+    resid,
+    resid_out,
+    row_w,
+    row_tab,
+    col_tab,
+    spread,
+    peak_out,
+    peak_all,
+    x_send,
+    x_recv,
+    meta_send,
+    meta_recv,
+    halo_send,
+    halo_recv,
+    row_send,
+    row_recv,
+    peak_send,
+    peak_recv,
+):
+    me, core = lax.axis_index("tm"), lax.axis_index("rows")
+    td = x_ref.shape[0]
+    rows = x_ref.shape[1]
+    total = n * td
+    f32, bf16 = jnp.float32, jnp.bfloat16
+
+    def peer(step):
+        return lax.rem(me + step, n)
+
+    def lanes_of(band):
+        return pl.ds(pl.multiple_of(band * LANES, LANES), LANES)
+
+    def x_copy(source, target):
+        return pltpu.make_async_remote_copy(
+            src_ref=x_ref.at[:, :, lanes_of(target)],
+            dst_ref=x_all.at[source],
+            send_sem=x_send.at[target],
+            recv_sem=x_recv.at[source],
+            device_id={"tm": target},
+            device_id_type=MESH,
+        )
+
+    def meta_copy(source, target):
+        return pltpu.make_async_remote_copy(
+            src_ref=meta_ref,
+            dst_ref=meta_all.at[source],
+            send_sem=meta_send.at[target],
+            recv_sem=meta_recv.at[source],
+            device_id={"tm": target},
+            device_id_type=MESH,
+        )
+
+    def halo_copy(source, target):
+        return pltpu.make_async_remote_copy(
+            src_ref=halo_out.at[target],
+            dst_ref=halo_all.at[source],
+            send_sem=halo_send.at[target],
+            recv_sem=halo_recv.at[source],
+            device_id={"tm": target},
+            device_id_type=MESH,
+        )
+
+    def row_copy(chunk):
+        return pltpu.make_async_remote_copy(
+            src_ref=resid_out.at[chunk],
+            dst_ref=resid.at[chunk, pl.ds(td * rows, td * HALO_ROWS)],
+            send_sem=row_send.at[chunk],
+            recv_sem=row_recv.at[chunk],
+            device_id={"rows": 1 - core},
+            device_id_type=MESH,
+        )
+
+    def peak_copy(source, target):
+        return pltpu.make_async_remote_copy(
+            src_ref=peak_out,
+            dst_ref=peak_all.at[source],
+            send_sem=peak_send.at[target],
+            recv_sem=peak_recv.at[source],
+            device_id={"tm": target},
+            device_id_type=MESH,
+        )
+
+    barrier = pltpu.get_barrier_semaphore()
+
+    def greet(step, carry):
+        pl.semaphore_signal(barrier, inc=1, device_id={"tm": peer(step)}, device_id_type=MESH)
+        return carry
+
+    lax.fori_loop(1, n, greet, 0)
+    pl.semaphore_signal(barrier, inc=1, device_id={"rows": 1 - core}, device_id_type=MESH)
+    pl.semaphore_wait(barrier, n)
+
+    def send_first(step, carry):
+        meta_copy(me, peer(step)).start()
+        x_copy(me, peer(step)).start()
+        return carry
+
+    lax.fori_loop(1, n, send_first, 0)
+
+    side = 2 * RADIUS
+    lane_in = lax.broadcasted_iota(jnp.int32, (LANES, 2 * LANES), 0)
+    lane_out = lax.broadcasted_iota(jnp.int32, (LANES, 2 * LANES), 1)
+    packed = jnp.zeros((n * rows, 2 * LANES), f32)
+    for j in range(td):
+        tiles = jnp.concatenate(
+            [x_ref[j, :, d * LANES : (d + 1) * LANES] for d in range(n)], axis=0
+        )
+        to_right = (lane_in >= LANES - RADIUS) & (
+            lane_out == lane_in - (LANES - RADIUS) + side * j
+        )
+        to_left = (lane_in < RADIUS) & (lane_out == LANES + lane_in + RADIUS + side * j)
+        packed = packed + jnp.dot(
+            tiles, (to_right | to_left).astype(f32).astype(bf16), preferred_element_type=f32
+        )
+    for d in range(n):
+        tile = jnp.zeros((rows, LANES), f32)
+        if d > 0:
+            tile = tile + packed[(d - 1) * rows : d * rows, :LANES]
+        if d < n - 1:
+            tile = tile + packed[(d + 1) * rows : (d + 2) * rows, LANES:]
+        halo_out[d] = tile.astype(bf16)
+
+    def send_halo(step, carry):
+        halo_copy(me, peer(step)).start()
+        return carry
+
+    lax.fori_loop(1, n, send_halo, 0)
+    meta_all[me] = meta_ref[...]
+    halo_all[me] = halo_out[me]
+    x_all[me] = x_ref[:, :, lanes_of(me)]
+
+    spread_in = lax.broadcasted_iota(jnp.int32, spread.shape, 0)
+    spread_out = lax.broadcasted_iota(jnp.int32, spread.shape, 1)
+    spread[...] = (
+        (spread_out % LANES < side) & (spread_in == side * (spread_out // LANES) + spread_out % LANES)
+    ).astype(f32).astype(bf16)
+    lane = lax.broadcasted_iota(jnp.int32, (2 * LANES, LANES), 0)
+    column = lax.broadcasted_iota(jnp.int32, (2 * LANES, LANES), 1)
+    source_col = jnp.where(
+        lane < LANES,
+        lane,
+        jnp.where(
+            lane < LANES + RADIUS,
+            lane - LANES - RADIUS,
+            jnp.where(lane < LANES + side, lane - RADIUS, 4 * LANES),
+        ),
+    )
+    column_offset = (source_col - column).astype(f32)
+    for s in range(WIDTHS):
+        col_tab[:, s * LANES : (s + 1) * LANES] = tap_values(column_offset, s + 1).astype(bf16)
+    out_row = lax.broadcasted_iota(jnp.int32, (rows, 2 * LANES), 0)
+    lane = lax.broadcasted_iota(jnp.int32, (rows, 2 * LANES), 1)
+    own = lane < td * rows
+    beside = lane - td * rows
+    time_of = jnp.where(own, lane // rows, beside // HALO_ROWS)
+    source_row = jnp.where(own, lane % rows, beside % HALO_ROWS + jnp.where(core == 0, rows, -HALO_ROWS))
+    row_offset = (source_row - out_row).astype(f32)
+    for s in range(WIDTHS):
+        values = tap_values(row_offset, s + 1).astype(bf16).astype(f32)
+        for j in range(td):
+            row_tab[s, j] = jnp.where(time_of == j, values, 0.0)
+    masked[0:HISTORY_FRAMES] = jnp.zeros((HISTORY_FRAMES,) + masked.shape[1:], f32)
+
+    def wait_meta(step, carry):
+        meta_copy(peer(step), me).wait_recv()
+        return carry
+
+    lax.fori_loop(1, n, wait_meta, 0)
+    meta = meta_all[...].reshape(total, LANES).astype(bf16)
+    entry = lax.broadcasted_iota(jnp.int32, (LANES, 2 * LANES), 0)
+    lane = lax.broadcasted_iota(jnp.int32, (LANES, 2 * LANES), 1)
+    tile_of = jnp.where(
+        lane < LANES,
+        me,
+        jnp.where(lane < LANES + RADIUS, me - 1, jnp.where(lane < LANES + side, me + 1, -1)),
+    )
+    inside = (tile_of >= 0) & (tile_of < n)
+    target = lax.broadcasted_iota(jnp.int32, (total, total), 0)
+    source = lax.broadcasted_iota(jnp.int32, (total, total), 1)
+    band = ((target - source >= 1) & (target - source <= HISTORY_FRAMES)).astype(f32).astype(bf16)
+    for rt in range(2):
+        pick = (inside & (entry == rt * n + tile_of)).astype(f32).astype(bf16)
+        keep = jnp.dot(meta, pick, preferred_element_type=f32)
+        counts = jnp.dot(band, keep.astype(bf16), preferred_element_type=f32)
+        keep_rows[rt] = keep
+        scale_rows[rt] = keep / jnp.maximum(counts, 1.0)
+    for f in range(2):
+        pick = (entry == 2 * n + f).astype(f32).astype(bf16)
+        width_rows[f] = jnp.dot(meta, pick, preferred_element_type=f32)
+
+    def residual_step(c, window):
+        @pl.when(c != me)
+        def _():
+            x_copy(c, me).wait_recv()
+            halo_copy(c, me).wait_recv()
+
+        first = pl.multiple_of(c * td, td)
+        halo = jnp.dot(halo_all[c], spread[...], preferred_element_type=f32)
+        keep = [keep_rows[rt, pl.ds(first, td), :] for rt in range(2)]
+        scale = [scale_rows[rt, pl.ds(first, td), :] for rt in range(2)]
+        window = list(window)
+        pending = None
+        for j in range(td):
+            pixels = jnp.concatenate(
+                [x_all[c, j].astype(f32), halo[:, j * LANES : (j + 1) * LANES]], axis=1
+            )
+            old = masked[first + j]
+            values, residuals = [], []
+            for rt in range(2):
+                part = slice(rt * TILE_R, (rt + 1) * TILE_R)
+                value = pixels[part] * keep[rt][j : j + 1]
+                residuals.append(value - window[rt] * scale[rt][j : j + 1])
+                window[rt] = window[rt] + (value - old[part])
+                values.append(value)
+            masked[first + j + HISTORY_FRAMES] = jnp.concatenate(values, axis=0)
+            resid[c, j * rows : (j + 1) * rows, :] = jnp.concatenate(residuals, axis=0).astype(bf16)
+            edge = jnp.where(core == 0, residuals[1], residuals[0])
+            if j % 2 == 0:
+                pending = edge
+            else:
+                at = (j // 2) * 2 * HALO_ROWS
+                resid_out[c, at : at + 2 * HALO_ROWS, :] = jnp.concatenate(
+                    [pending, edge], axis=0
+                ).astype(bf16)
+        row_copy(c).start()
+        return tuple(window)
+
+    blank = jnp.zeros((TILE_R, 2 * LANES), f32)
+    lax.fori_loop(0, n, residual_step, (blank, blank))
+
+    def filter_step(c, totals):
+        row_copy(c).wait_recv()
+        first = pl.multiple_of(c * td, td)
+        excess, peak = list(totals[:2]), list(totals[2:])
+        width = [width_rows[f, pl.ds(first, td), :] for f in range(2)]
+        for j in range(td):
+            for f in range(2):
+                at = (2 * j + f) * rows
+                chosen = jnp.broadcast_to(width[f][j : j + 1], (rows, 2 * LANES))
+                row_w[at : at + rows, :] = pick_width(
+                    chosen, [row_tab[s, j] for s in range(WIDTHS)]
+                ).astype(bf16)
+        row_result = jnp.dot(
+            row_w[:, : td * (rows + HALO_ROWS)], resid[c], preferred_element_type=f32
+        ).astype(bf16)
+        trial = jnp.dot(row_result, col_tab[...], preferred_element_type=f32)
+        for j in range(td):
+            for f in range(2):
+                at = (2 * j + f) * rows
+                chosen = jnp.broadcast_to(width[f][j : j + 1, :LANES], (rows, LANES))
+                filtered = pick_width(
+                    chosen,
+                    [
+                        trial[at : at + rows, s * LANES : (s + 1) * LANES]
+                        for s in range(WIDTHS)
+                    ],
+                )
+                excess[f] = excess[f] + jnp.maximum(filtered - threshold, 0.0)
+                peak[f] = jnp.maximum(peak[f], filtered)
+        return tuple(excess) + tuple(peak)
+
+    zero = jnp.zeros((rows, LANES), f32)
+    low = jnp.full((rows, LANES), -1e30, f32)
+    results = lax.fori_loop(0, n, filter_step, (zero, zero, low, low))
+    for f in range(2):
+        peak_out[f] = results[2 + f].astype(bf16)
+
+    def send_peak(step, carry):
+        peak_copy(me, peer(step)).start()
+        return carry
+
+    lax.fori_loop(1, n, send_peak, 0)
+    peak_all[me] = peak_out[...]
+    for f in range(2):
+        exc_ref[f] = results[f] * (1.0 / total)
+
+    def finish_sends(step, carry):
+        target = peer(step)
+        x_copy(me, target).wait_send()
+        meta_copy(me, target).wait_send()
+        halo_copy(me, target).wait_send()
+        return carry
+
+    lax.fori_loop(1, n, finish_sends, 0)
+
+    def finish_rows(c, carry):
+        row_copy(c).wait_send()
+        return carry
+
+    lax.fori_loop(0, n, finish_rows, 0)
+
+    def finish_peaks(step, carry):
+        source = peer(step)
+        peak_copy(source, me).wait_recv()
+        peak_copy(me, source).wait_send()
+        return carry
+
+    lax.fori_loop(1, n, finish_peaks, 0)
+    for d in range(n):
+        peak_ref[:, :, d * LANES : (d + 1) * LANES] = peak_all[d].astype(f32)
+
+
+def fused_body(n, snapshots, tile_masks, widths):
+    td, rows, cols = snapshots.shape
+    total = n * td
+    filters = widths.shape[1]
+    flat = tile_masks.reshape(td, -1)
+    meta = jnp.concatenate([flat, widths], axis=1).astype(jnp.float32)
+    meta = jnp.pad(meta, ((0, 0), (0, LANES - meta.shape[1])))
+    f32, bf16 = jnp.float32, jnp.bfloat16
+    depth = td * (rows + HALO_ROWS)
+    dma = pltpu.SemaphoreType.DMA((n,))
+    return pl.pallas_call(
+        functools.partial(search_kernel, n),
+        out_shape=(
+            jax.ShapeDtypeStruct((filters, rows, LANES), f32),
+            jax.ShapeDtypeStruct((filters, rows, cols), f32),
+        ),
+        in_specs=[pl.BlockSpec(memory_space=pltpu.VMEM)] * 2,
+        out_specs=(pl.BlockSpec(memory_space=pltpu.VMEM),) * 2,
+        scratch_shapes=[
+            pltpu.VMEM((n, td, rows, LANES), bf16),
+            pltpu.VMEM((n, rows, LANES), bf16),
+            pltpu.VMEM((n, rows, LANES), bf16),
+            pltpu.VMEM((n, td, LANES), f32),
+            pltpu.VMEM((2, total, 2 * LANES), f32),
+            pltpu.VMEM((2, total, 2 * LANES), f32),
+            pltpu.VMEM((filters, total, 2 * LANES), f32),
+            pltpu.VMEM((total + HISTORY_FRAMES, rows, 2 * LANES), f32),
+            pltpu.VMEM((n, depth, 2 * LANES), bf16),
+            pltpu.VMEM((n, td * HALO_ROWS, 2 * LANES), bf16),
+            pltpu.VMEM((td * filters * rows, 2 * LANES), bf16),
+            pltpu.VMEM((WIDTHS, td, rows, 2 * LANES), f32),
+            pltpu.VMEM((2 * LANES, WIDTHS * LANES), bf16),
+            pltpu.VMEM((LANES, td * LANES), bf16),
+            pltpu.VMEM((filters, rows, LANES), bf16),
+            pltpu.VMEM((n, filters, rows, LANES), bf16),
+        ]
+        + [dma] * 10,
+        compiler_params=pltpu.CompilerParams(
+            collective_id=0, has_side_effects=True, vmem_limit_bytes=40 * 2**20
+        ),
+    )(snapshots, meta)
+
+
 def solution(mesh):
+    count = mesh.shape["tm"]
+
+    def per_device(snapshots, tile_masks, widths):
+        td, rows, cols = snapshots.shape
+        fits = (
+            mesh.shape["rows"] == 2
+            and (td, rows, widths.shape[1]) == (8, 2 * TILE_R, 2)
+            and cols == count * LANES
+            and 2 * count + 2 <= LANES
+        )
+        if fits:
+            return fused_body(count, snapshots, tile_masks, widths)
+        return body(snapshots, tile_masks, widths)
+
     return jax.shard_map(
-        body,
+        per_device,
         mesh=mesh,
         in_specs=(P("tm", "rows", None), P("tm", "rows", None), P("tm", None)),
         out_specs=(P(None, "rows", "tm"), P(None, "rows", None)),

time: 192 us -> 41.5 us (0.22)
  blocking collectives: 119 us -> 0 us
  Pallas kernels: 0 us -> 37.4 us
  local copies, waits for them, and re-layouts: 29.4 us -> 3.22 us
  matrix products: 21.9 us -> 0 us
  starting transfers between devices: 14.7 us -> 0 us
  other arithmetic: 4.06 us -> 0.08 us
    all_gather x3 -> x0, blocking collectives: 119 us -> none  [the longest x1 43.1 us: column_residual(): lax.all_gather(tile_masks, 'tm', axis=0, tiled=True)]
    pallas_call x0 -> x1, Pallas kernels: none -> 37.4 us  [fused_body(): pl.pallas_call(functools.partial(search_kernel, n), out_shape=(jax.ShapeD...]
    dot_general x13 -> x0, matrix products: 21.9 us -> none  [the longest x2 10.9 us: body(): jnp.einsum('trj,tjc->trc', padded_cols[filter_index], column_weights, pre...]
    unnamed x22 -> x7, local copies, waits for them, and re-layouts: 18.1 us -> 2.44 us
    all_to_all x1 -> x0, starting transfers between devices: 8.44 us -> none  [column_residual(): lax.all_to_all(snapshots, 'tm', split_axis=2, concat_axis=0, tiled=True)]
    ppermute x4 -> x0, starting transfers between devices: 6.26 us -> none  [the longest x2 3.37 us: padded(): before = lax.ppermute(last, axis, up)]
    all_to_all x1 -> x0, local copies, waits for them, and re-layouts: 4.41 us -> none  [column_residual(): lax.all_to_all(snapshots, 'tm', split_axis=2, concat_axis=0, tiled=True)]
    convert_element_type x7 -> x0, local copies, waits for them, and re-layouts: 3.1 us -> none  [the longest x2 2.4 us: body(): row_weights = jnp.einsum('jik,tk->tij', row_onehot, kernel[:, filter_inde...]
  transfers between devices with their start and end apart: 5 -> 0, of which waited for: 1 -> 0; matrix products, arithmetic and copies ran while one was open for 8% -> 0% of each run, Pallas kernels for 0% -> 0%
where the time goes in v1:
time: 41.5 us; the launch traced here: 41.3 us
  Pallas kernels  37.4 us (90%)
  local copies, waits for them, and re-layouts  3.22 us (8%)
  between operations  0.65 us (2%)
    pallas_call x1, Pallas kernels, fused_body(): pl.pallas_call(functools.partial(search_kernel, n), out_shape=(jax.ShapeD...  37.4 us
    unnamed x7, local copies, waits for them, and re-layouts  2.44 us

profile of v1, /device:TPU:0, one launch (start us, length us, event | category | flops | bytes accessed | tf_op | source)
XLA Modules:
  0.0 41.3 jit_solution(6608432057227855898)
XLA Ops:
  0.6 0.0 copy-start.1
  0.6 0.8 %reshape.7 = s32[8,32]{1,0:T(8,128)S(1)} reshape(s32[8,2,16]{2,1,0:T(2,128)} %param.4) | data formatting | bytes 2048 | tf_op jit(solution)/shard_map/reshape | solution.py:472
  1.4 0.0 copy-done.1
  1.4 0.1 copy.5
  1.5 0.1 add_convert_fusion
  1.6 0.0 copy-start
  1.6 1.0 %copy-done = bf16[8,16,2048]{2,1,0:T(8,128)(2,1)S(1)} copy-done((bf16[8,16,2048]{2,1,0:T(8,128)(2,1)S(1)}, bf16[8,16,2048]{2,1,0:T(8,128)(2,1)}, u32[]{:S(2)}) %copy-start) | copy-done | bytes 524312
  2.6 37.4 %shard_map.50 = (f32[2,16,128]{2,1,0:T(8,128)S(1)}, f32[2,16,2048]{2,1,0:T(8,128)S(1)}) custom-call(bf16[8,16,2048]{2,1,0:T(8,128)(2,1)S(1)} %copy-done, f32[8,128]{1,0:T(8,128)S(1)} %pad.4.meta_ref), custom_call_target="tpu_custom_call" | custom-call | tf_op jit(solution)/shard_map/pallas_call | solution.py:478
  40.0 0.6 %copy.8 = f32[2,16,128]{2,1,0:T(8,128)} copy(f32[2,16,128]{2,1,0:T(8,128)S(1)} %get-tuple-element.4) | data formatting | bytes 32768
  40.6 0.7 %copy.9 = f32[2,16,2048]{2,1,0:T(8,128)} copy(f32[2,16,2048]{2,1,0:T(8,128)S(1)} %get-tuple-element.5) | data formatting | bytes 524288
  (1 shorter events, 0.0 us)
Async XLA Ops:
  0.6 0.8 %copy-start.1 = (s32[8,2]{0,1:T(2,128)S(1)}, s32[8,2]{0,1:T(2,128)}, u32[]{:S(2)}) copy-start(s32[8,2]{0,1:T(2,128)} %param.5) | copy-start | bytes 196
  1.6 1.0 %copy-start = (bf16[8,16,2048]{2,1,0:T(8,128)(2,1)S(1)}, bf16[8,16,2048]{2,1,0:T(8,128)(2,1)}, u32[]{:S(2)}) copy-start(bf16[8,16,2048]{2,1,0:T(8,128)(2,1)} %x_ref.1) | copy-start | bytes 1572868

commit v2 on v1

--- a/solution.py
+++ b/solution.py
@@ -152,10 +152,13 @@
 
 def search_kernel(
     n,
+    x_hbm,
+    flags_ref,
+    widths_ref,
+    exc_ref,
+    peak_ref,
     x_ref,
     meta_ref,
-    exc_ref,
-    peak_ref,
     x_all,
     halo_out,
     halo_all,
@@ -182,6 +185,7 @@
     row_recv,
     peak_send,
     peak_recv,
+    load_sem,
 ):
     me, core = lax.axis_index("tm"), lax.axis_index("rows")
     td = x_ref.shape[0]
@@ -190,7 +194,7 @@
     f32, bf16 = jnp.float32, jnp.bfloat16
 
     def peer(step):
-        return lax.rem(me + step, n)
+        return lax.rem(me + n - step, n)
 
     def lanes_of(band):
         return pl.ds(pl.multiple_of(band * LANES, LANES), LANES)
@@ -245,6 +249,8 @@
             device_id_type=MESH,
         )
 
+    load = pltpu.make_async_copy(x_hbm, x_ref, load_sem)
+    load.start()
     barrier = pltpu.get_barrier_semaphore()
 
     def greet(step, carry):
@@ -253,6 +259,12 @@
 
     lax.fori_loop(1, n, greet, 0)
     pl.semaphore_signal(barrier, inc=1, device_id={"rows": 1 - core}, device_id_type=MESH)
+    meta_ref[...] = jnp.zeros_like(meta_ref)
+    for j in range(td):
+        for rt in range(2):
+            meta_ref[j : j + 1, rt * n : (rt + 1) * n] = flags_ref[j, rt : rt + 1, :].astype(f32)
+    meta_ref[:, 2 * n : 2 * n + 2] = widths_ref[...].astype(f32)
+    load.wait()
     pl.semaphore_wait(barrier, n)
 
     def send_first(step, carry):
@@ -352,6 +364,20 @@
     for f in range(2):
         pick = (entry == 2 * n + f).astype(f32).astype(bf16)
         width_rows[f] = jnp.dot(meta, pick, preferred_element_type=f32)
+
+    def weight_step(c, carry):
+        first = pl.multiple_of(c * td, td)
+        width = [width_rows[f, pl.ds(first, td), :] for f in range(2)]
+        for j in range(td):
+            for f in range(2):
+                at = (2 * j + f) * rows
+                chosen = jnp.broadcast_to(width[f][j : j + 1], (rows, 2 * LANES))
+                row_w[c, at : at + rows, :] = pick_width(
+                    chosen, [row_tab[s, j] for s in range(WIDTHS)]
+                ).astype(bf16)
+        return carry
+
+    lax.fori_loop(0, n, weight_step, 0)
 
     def residual_step(c, window):
         @pl.when(c != me)
@@ -391,22 +417,15 @@
         return tuple(window)
 
     blank = jnp.zeros((TILE_R, 2 * LANES), f32)
-    lax.fori_loop(0, n, residual_step, (blank, blank))
+    window = residual_step(0, (blank, blank))
 
     def filter_step(c, totals):
         row_copy(c).wait_recv()
         first = pl.multiple_of(c * td, td)
         excess, peak = list(totals[:2]), list(totals[2:])
         width = [width_rows[f, pl.ds(first, td), :] for f in range(2)]
-        for j in range(td):
-            for f in range(2):
-                at = (2 * j + f) * rows
-                chosen = jnp.broadcast_to(width[f][j : j + 1], (rows, 2 * LANES))
-                row_w[at : at + rows, :] = pick_width(
-                    chosen, [row_tab[s, j] for s in range(WIDTHS)]
-                ).astype(bf16)
         row_result = jnp.dot(
-            row_w[:, : td * (rows + HALO_ROWS)], resid[c], preferred_element_type=f32
+            row_w[c, :, : td * (rows + HALO_ROWS)], resid[c], preferred_element_type=f32
         ).astype(bf16)
         trial = jnp.dot(row_result, col_tab[...], preferred_element_type=f32)
         for j in range(td):
@@ -426,7 +445,13 @@
 
     zero = jnp.zeros((rows, LANES), f32)
     low = jnp.full((rows, LANES), -1e30, f32)
-    results = lax.fori_loop(0, n, filter_step, (zero, zero, low, low))
+
+    def both(c, carry):
+        window = residual_step(c, carry[:2])
+        return window + filter_step(c - 1, carry[2:])
+
+    carry = lax.fori_loop(1, n, both, window + (zero, zero, low, low))
+    results = filter_step(n - 1, carry[2:])
     for f in range(2):
         peak_out[f] = results[2 + f].astype(bf16)
 
@@ -469,9 +494,6 @@
     td, rows, cols = snapshots.shape
     total = n * td
     filters = widths.shape[1]
-    flat = tile_masks.reshape(td, -1)
-    meta = jnp.concatenate([flat, widths], axis=1).astype(jnp.float32)
-    meta = jnp.pad(meta, ((0, 0), (0, LANES - meta.shape[1])))
     f32, bf16 = jnp.float32, jnp.bfloat16
     depth = td * (rows + HALO_ROWS)
     dma = pltpu.SemaphoreType.DMA((n,))
@@ -481,9 +503,15 @@
             jax.ShapeDtypeStruct((filters, rows, LANES), f32),
             jax.ShapeDtypeStruct((filters, rows, cols), f32),
         ),
-        in_specs=[pl.BlockSpec(memory_space=pltpu.VMEM)] * 2,
+        in_specs=[
+            pl.BlockSpec(memory_space=pl.ANY),
+            pl.BlockSpec(memory_space=pltpu.VMEM),
+            pl.BlockSpec(memory_space=pltpu.VMEM),
+        ],
         out_specs=(pl.BlockSpec(memory_space=pltpu.VMEM),) * 2,
         scratch_shapes=[
+            pltpu.VMEM((td, rows, cols), bf16),
+            pltpu.VMEM((td, LANES), f32),
             pltpu.VMEM((n, td, rows, LANES), bf16),
             pltpu.VMEM((n, rows, LANES), bf16),
             pltpu.VMEM((n, rows, LANES), bf16),
@@ -494,18 +522,19 @@
             pltpu.VMEM((total + HISTORY_FRAMES, rows, 2 * LANES), f32),
             pltpu.VMEM((n, depth, 2 * LANES), bf16),
             pltpu.VMEM((n, td * HALO_ROWS, 2 * LANES), bf16),
-            pltpu.VMEM((td * filters * rows, 2 * LANES), bf16),
+            pltpu.VMEM((n, td * filters * rows, 2 * LANES), bf16),
             pltpu.VMEM((WIDTHS, td, rows, 2 * LANES), f32),
             pltpu.VMEM((2 * LANES, WIDTHS * LANES), bf16),
             pltpu.VMEM((LANES, td * LANES), bf16),
             pltpu.VMEM((filters, rows, LANES), bf16),
             pltpu.VMEM((n, filters, rows, LANES), bf16),
         ]
-        + [dma] * 10,
+        + [dma] * 10
+        + [pltpu.SemaphoreType.DMA],
         compiler_params=pltpu.CompilerParams(
             collective_id=0, has_side_effects=True, vmem_limit_bytes=40 * 2**20
         ),
-    )(snapshots, meta)
+    )(snapshots, tile_masks, widths)
 
 
 def solution(mesh):

time: 41.5 us -> 45.7 us (1.10)
  Pallas kernels: 37.4 us -> 41.1 us
  local copies, waits for them, and re-layouts: 3.22 us -> 3.8 us
    pallas_call x1, Pallas kernels: 37.4 us -> 41.1 us  [fused_body(): pl.pallas_call(functools.partial(search_kernel, n), out_shape=(jax.ShapeD...]
    unnamed x7, local copies, waits for them, and re-layouts: 2.44 us -> 3.8 us
    reshape x1 -> x0, local copies, waits for them, and re-layouts: 0.78 us -> none  [fused_body(): flat = tile_masks.reshape(td, -1)]
where the time goes in v2:
time: 45.7 us; the launch traced here: 45.5 us
  Pallas kernels  41.1 us (90%)
  local copies, waits for them, and re-layouts  3.8 us (8%)
  between operations  0.64 us (1%)
    pallas_call x1, Pallas kernels, fused_body(): pl.pallas_call(functools.partial(search_kernel, n), out_shape=(jax.ShapeD...  41.1 us
    unnamed x7, local copies, waits for them, and re-layouts  3.8 us

profile of v2, /device:TPU:0, one launch (start us, length us, event | category | flops | bytes accessed | tf_op | source)
XLA Modules:
  0.0 45.5 jit_solution(17804415772262819761)
XLA Ops:
  0.6 0.8 %copy.5.widths_ref = s32[8,2]{1,0:T(8,128)S(1)} copy(s32[8,2]{0,1:T(2,128)} %param.5) | data formatting | bytes 128 | tf_op args[2]
  1.4 0.0 copy-start
  1.4 1.0 %copy-done = bf16[8,16,2048]{2,1,0:T(8,128)(2,1)S(1)} copy-done((bf16[8,16,2048]{2,1,0:T(8,128)(2,1)S(1)}, bf16[8,16,2048]{2,1,0:T(8,128)(2,1)}, u32[]{:S(2)}) %copy-start) | copy-done | bytes 524312
  2.4 0.0 copy-start.1
  2.4 0.7 %copy-done.1 = s32[8,2,16]{2,1,0:T(2,128)S(1)} copy-done((s32[8,2,16]{2,1,0:T(2,128)S(1)}, s32[8,2,16]{2,1,0:T(2,128)}, u32[]{:S(2)}) %copy-start.1) | copy-done | bytes 1048
  3.1 41.1 %shard_map.50 = (f32[2,16,128]{2,1,0:T(8,128)S(1)}, f32[2,16,2048]{2,1,0:T(8,128)S(1)}) custom-call(bf16[8,16,2048]{2,1,0:T(8,128)(2,1)S(1)} %copy-done, s32[8,2,16]{2,1,0:T(2,128)S(1)} %copy-done.1, s32[8,2]{1,0:T(8,128)S(1)} %copy.5.widths_ref), custom_call_target="tpu_custom_call" | custom-call | tf_op jit(solution)/shard_map/pallas_call | solution.py:500
  44.2 0.6 %copy.8 = f32[2,16,128]{2,1,0:T(8,128)} copy(f32[2,16,128]{2,1,0:T(8,128)S(1)} %get-tuple-element.4) | data formatting | bytes 32768
  44.8 0.7 %copy.9 = f32[2,16,2048]{2,1,0:T(8,128)} copy(f32[2,16,2048]{2,1,0:T(8,128)S(1)} %get-tuple-element.5) | data formatting | bytes 524288
Async XLA Ops:
  1.4 1.0 %copy-start = (bf16[8,16,2048]{2,1,0:T(8,128)(2,1)S(1)}, bf16[8,16,2048]{2,1,0:T(8,128)(2,1)}, u32[]{:S(2)}) copy-start(bf16[8,16,2048]{2,1,0:T(8,128)(2,1)} %x_hbm.1) | copy-start | bytes 1572868
  2.4 0.7 %copy-start.1 = (s32[8,2,16]{2,1,0:T(2,128)S(1)}, s32[8,2,16]{2,1,0:T(2,128)}, u32[]{:S(2)}) copy-start(s32[8,2,16]{2,1,0:T(2,128)} %flags_ref.1) | copy-start | bytes 3076

commit v3 on v1

--- a/solution.py
+++ b/solution.py
@@ -190,7 +190,7 @@
     f32, bf16 = jnp.float32, jnp.bfloat16
 
     def peer(step):
-        return lax.rem(me + step, n)
+        return lax.rem(me + n - step, n)
 
     def lanes_of(band):
         return pl.ds(pl.multiple_of(band * LANES, LANES), LANES)
@@ -352,6 +352,20 @@
     for f in range(2):
         pick = (entry == 2 * n + f).astype(f32).astype(bf16)
         width_rows[f] = jnp.dot(meta, pick, preferred_element_type=f32)
+
+    def weight_step(c, carry):
+        first = pl.multiple_of(c * td, td)
+        width = [width_rows[f, pl.ds(first, td), :] for f in range(2)]
+        for j in range(td):
+            for f in range(2):
+                at = (2 * j + f) * rows
+                chosen = jnp.broadcast_to(width[f][j : j + 1], (rows, 2 * LANES))
+                row_w[c, at : at + rows, :] = pick_width(
+                    chosen, [row_tab[s, j] for s in range(WIDTHS)]
+                ).astype(bf16)
+        return carry
+
+    lax.fori_loop(0, n, weight_step, 0)
 
     def residual_step(c, window):
         @pl.when(c != me)
@@ -393,40 +407,42 @@
     blank = jnp.zeros((TILE_R, 2 * LANES), f32)
     lax.fori_loop(0, n, residual_step, (blank, blank))
 
-    def filter_step(c, totals):
-        row_copy(c).wait_recv()
-        first = pl.multiple_of(c * td, td)
+    def filter_step(g, totals):
         excess, peak = list(totals[:2]), list(totals[2:])
-        width = [width_rows[f, pl.ds(first, td), :] for f in range(2)]
-        for j in range(td):
-            for f in range(2):
-                at = (2 * j + f) * rows
-                chosen = jnp.broadcast_to(width[f][j : j + 1], (rows, 2 * LANES))
-                row_w[at : at + rows, :] = pick_width(
-                    chosen, [row_tab[s, j] for s in range(WIDTHS)]
+        row_results, width = [], []
+        for part in range(group):
+            c = g * group + part
+            row_copy(c).wait_recv()
+            first = pl.multiple_of(c * td, td)
+            width.append([width_rows[f, pl.ds(first, td), :] for f in range(2)])
+            row_results.append(
+                jnp.dot(
+                    row_w[c, :, : td * (rows + HALO_ROWS)], resid[c], preferred_element_type=f32
                 ).astype(bf16)
-        row_result = jnp.dot(
-            row_w[:, : td * (rows + HALO_ROWS)], resid[c], preferred_element_type=f32
-        ).astype(bf16)
-        trial = jnp.dot(row_result, col_tab[...], preferred_element_type=f32)
-        for j in range(td):
-            for f in range(2):
-                at = (2 * j + f) * rows
-                chosen = jnp.broadcast_to(width[f][j : j + 1, :LANES], (rows, LANES))
-                filtered = pick_width(
-                    chosen,
-                    [
-                        trial[at : at + rows, s * LANES : (s + 1) * LANES]
-                        for s in range(WIDTHS)
-                    ],
-                )
-                excess[f] = excess[f] + jnp.maximum(filtered - threshold, 0.0)
-                peak[f] = jnp.maximum(peak[f], filtered)
+            )
+        trial = jnp.dot(
+            jnp.concatenate(row_results, axis=0), col_tab[...], preferred_element_type=f32
+        )
+        for part in range(group):
+            for j in range(td):
+                for f in range(2):
+                    at = ((part * td + j) * 2 + f) * rows
+                    chosen = jnp.broadcast_to(width[part][f][j : j + 1, :LANES], (rows, LANES))
+                    filtered = pick_width(
+                        chosen,
+                        [
+                            trial[at : at + rows, s * LANES : (s + 1) * LANES]
+                            for s in range(WIDTHS)
+                        ],
+                    )
+                    excess[f] = excess[f] + jnp.maximum(filtered - threshold, 0.0)
+                    peak[f] = jnp.maximum(peak[f], filtered)
         return tuple(excess) + tuple(peak)
 
+    group = 4 if n % 4 == 0 else 1
     zero = jnp.zeros((rows, LANES), f32)
     low = jnp.full((rows, LANES), -1e30, f32)
-    results = lax.fori_loop(0, n, filter_step, (zero, zero, low, low))
+    results = lax.fori_loop(0, n // group, filter_step, (zero, zero, low, low))
     for f in range(2):
         peak_out[f] = results[2 + f].astype(bf16)
 
@@ -494,7 +510,7 @@
             pltpu.VMEM((total + HISTORY_FRAMES, rows, 2 * LANES), f32),
             pltpu.VMEM((n, depth, 2 * LANES), bf16),
             pltpu.VMEM((n, td * HALO_ROWS, 2 * LANES), bf16),
-            pltpu.VMEM((td * filters * rows, 2 * LANES), bf16),
+            pltpu.VMEM((n, td * filters * rows, 2 * LANES), bf16),
             pltpu.VMEM((WIDTHS, td, rows, 2 * LANES), f32),
             pltpu.VMEM((2 * LANES, WIDTHS * LANES), bf16),
             pltpu.VMEM((LANES, td * LANES), bf16),

time: 41.5 us -> 40.7 us (0.981)
  Pallas kernels: 37.4 us -> 36.5 us
    pallas_call x1, Pallas kernels: 37.4 us -> 36.5 us  [fused_body(): pl.pallas_call(functools.partial(search_kernel, n), out_shape=(jax.ShapeD...]
where the time goes in v3:
time: 40.7 us; the launch traced here: 40.5 us
  Pallas kernels  36.5 us (90%)
  local copies, waits for them, and re-layouts  3.22 us (8%)
  between operations  0.65 us (2%)
    pallas_call x1, Pallas kernels, fused_body(): pl.pallas_call(functools.partial(search_kernel, n), out_shape=(jax.ShapeD...  36.5 us
    unnamed x7, local copies, waits for them, and re-layouts  2.44 us

profile of v3, /device:TPU:0, one launch (start us, length us, event | category | flops | bytes accessed | tf_op | source)
XLA Modules:
  0.0 40.5 jit_solution(478293638323027873)
XLA Ops:
  0.6 0.0 copy-start.1
  0.6 0.8 %reshape.7 = s32[8,32]{1,0:T(8,128)S(1)} reshape(s32[8,2,16]{2,1,0:T(2,128)} %param.4) | data formatting | bytes 2048 | tf_op jit(solution)/shard_map/reshape | solution.py:488
  1.4 0.0 copy-done.1
  1.4 0.1 copy.5
  1.5 0.1 add_convert_fusion
  1.6 0.0 copy-start
  1.6 1.0 %copy-done = bf16[8,16,2048]{2,1,0:T(8,128)(2,1)S(1)} copy-done((bf16[8,16,2048]{2,1,0:T(8,128)(2,1)S(1)}, bf16[8,16,2048]{2,1,0:T(8,128)(2,1)}, u32[]{:S(2)}) %copy-start) | copy-done | bytes 524312
  2.6 36.5 %shard_map.50 = (f32[2,16,128]{2,1,0:T(8,128)S(1)}, f32[2,16,2048]{2,1,0:T(8,128)S(1)}) custom-call(bf16[8,16,2048]{2,1,0:T(8,128)(2,1)S(1)} %copy-done, f32[8,128]{1,0:T(8,128)S(1)} %pad.4.meta_ref), custom_call_target="tpu_custom_call" | custom-call | tf_op jit(solution)/shard_map/pallas_call | solution.py:494
  39.2 0.6 %copy.8 = f32[2,16,128]{2,1,0:T(8,128)} copy(f32[2,16,128]{2,1,0:T(8,128)S(1)} %get-tuple-element.4) | data formatting | bytes 32768
  39.8 0.7 %copy.9 = f32[2,16,2048]{2,1,0:T(8,128)} copy(f32[2,16,2048]{2,1,0:T(8,128)S(1)} %get-tuple-element.5) | data formatting | bytes 524288
  (1 shorter events, 0.0 us)
Async XLA Ops:
  0.6 0.8 %copy-start.1 = (s32[8,2]{0,1:T(2,128)S(1)}, s32[8,2]{0,1:T(2,128)}, u32[]{:S(2)}) copy-start(s32[8,2]{0,1:T(2,128)} %param.5) | copy-start | bytes 196
  1.6 1.0 %copy-start = (bf16[8,16,2048]{2,1,0:T(8,128)(2,1)S(1)}, bf16[8,16,2048]{2,1,0:T(8,128)(2,1)}, u32[]{:S(2)}) copy-start(bf16[8,16,2048]{2,1,0:T(8,128)(2,1)} %x_ref.1) | copy-start | bytes 1572868

commit v4 on v3

--- a/solution.py
+++ b/solution.py
@@ -257,10 +257,15 @@
 
     def send_first(step, carry):
         meta_copy(me, peer(step)).start()
+        return carry
+
+    lax.fori_loop(1, n, send_first, 0)
+
+    def send_pixels(step, carry):
         x_copy(me, peer(step)).start()
         return carry
 
-    lax.fori_loop(1, n, send_first, 0)
+    lax.fori_loop(1, n, send_pixels, 0)
 
     side = 2 * RADIUS
     lane_in = lax.broadcasted_iota(jnp.int32, (LANES, 2 * LANES), 0)

time: 40.7 us -> 40.6 us (level)
  no operation moved by 1% of the time
where the time goes in v4:
time: 40.6 us; the launch traced here: 40.4 us
  Pallas kernels  36.5 us (90%)
  local copies, waits for them, and re-layouts  3.22 us (8%)
  between operations  0.65 us (2%)
    pallas_call x1, Pallas kernels, fused_body(): pl.pallas_call(functools.partial(search_kernel, n), out_shape=(jax.ShapeD...  36.5 us
    unnamed x7, local copies, waits for them, and re-layouts  2.44 us

profile of v4, /device:TPU:0, one launch (start us, length us, event | category | flops | bytes accessed | tf_op | source)
XLA Modules:
  0.0 40.4 jit_solution(10450911949589798818)
XLA Ops:
  0.6 0.0 copy-start.1
  0.6 0.8 %reshape.7 = s32[8,32]{1,0:T(8,128)S(1)} reshape(s32[8,2,16]{2,1,0:T(2,128)} %param.4) | data formatting | bytes 2048 | tf_op jit(solution)/shard_map/reshape | solution.py:493
  1.4 0.0 copy-done.1
  1.4 0.1 copy.5
  1.5 0.1 add_convert_fusion
  1.6 0.0 copy-start
  1.6 1.0 %copy-done = bf16[8,16,2048]{2,1,0:T(8,128)(2,1)S(1)} copy-done((bf16[8,16,2048]{2,1,0:T(8,128)(2,1)S(1)}, bf16[8,16,2048]{2,1,0:T(8,128)(2,1)}, u32[]{:S(2)}) %copy-start) | copy-done | bytes 524312
  2.6 36.5 %shard_map.50 = (f32[2,16,128]{2,1,0:T(8,128)S(1)}, f32[2,16,2048]{2,1,0:T(8,128)S(1)}) custom-call(bf16[8,16,2048]{2,1,0:T(8,128)(2,1)S(1)} %copy-done, f32[8,128]{1,0:T(8,128)S(1)} %pad.4.meta_ref), custom_call_target="tpu_custom_call" | custom-call | tf_op jit(solution)/shard_map/pallas_call | solution.py:499
  39.1 0.6 %copy.8 = f32[2,16,128]{2,1,0:T(8,128)} copy(f32[2,16,128]{2,1,0:T(8,128)S(1)} %get-tuple-element.4) | data formatting | bytes 32768
  39.7 0.7 %copy.9 = f32[2,16,2048]{2,1,0:T(8,128)} copy(f32[2,16,2048]{2,1,0:T(8,128)S(1)} %get-tuple-element.5) | data formatting | bytes 524288
  (1 shorter events, 0.0 us)
Async XLA Ops:
  0.6 0.8 %copy-start.1 = (s32[8,2]{0,1:T(2,128)S(1)}, s32[8,2]{0,1:T(2,128)}, u32[]{:S(2)}) copy-start(s32[8,2]{0,1:T(2,128)} %param.5) | copy-start | bytes 196
  1.6 1.0 %copy-start = (bf16[8,16,2048]{2,1,0:T(8,128)(2,1)S(1)}, bf16[8,16,2048]{2,1,0:T(8,128)(2,1)}, u32[]{:S(2)}) copy-start(bf16[8,16,2048]{2,1,0:T(8,128)(2,1)} %x_ref.1) | copy-start | bytes 1572868

commit v5 on v4

--- a/solution.py
+++ b/solution.py
@@ -410,7 +410,6 @@
         return tuple(window)
 
     blank = jnp.zeros((TILE_R, 2 * LANES), f32)
-    lax.fori_loop(0, n, residual_step, (blank, blank))
 
     def filter_step(g, totals):
         excess, peak = list(totals[:2]), list(totals[2:])
@@ -447,7 +446,18 @@
     group = 4 if n % 4 == 0 else 1
     zero = jnp.zeros((rows, LANES), f32)
     low = jnp.full((rows, LANES), -1e30, f32)
-    results = lax.fori_loop(0, n // group, filter_step, (zero, zero, low, low))
+
+    def residual_group(g, window):
+        return lax.fori_loop(
+            0, group, lambda part, carry: residual_step(g * group + part, carry), window
+        )
+
+    def both(g, carry):
+        return residual_group(g, carry[:2]) + filter_step(g - 1, carry[2:])
+
+    carry = residual_group(0, (blank, blank)) + (zero, zero, low, low)
+    carry = lax.fori_loop(1, n // group, both, carry)
+    results = filter_step(n // group - 1, carry[2:])
     for f in range(2):
         peak_out[f] = results[2 + f].astype(bf16)
 

time: 40.6 us -> 40.9 us (level)
  no operation moved by 1% of the time
where the time goes in v5:
time: 40.9 us; the launch traced here: 40.7 us
  Pallas kernels  36.7 us (90%)
  local copies, waits for them, and re-layouts  3.22 us (8%)
  between operations  0.65 us (2%)
    pallas_call x1, Pallas kernels, fused_body(): pl.pallas_call(functools.partial(search_kernel, n), out_shape=(jax.ShapeD...  36.7 us
    unnamed x7, local copies, waits for them, and re-layouts  2.44 us

profile of v5, /device:TPU:0, one launch (start us, length us, event | category | flops | bytes accessed | tf_op | source)
XLA Modules:
  0.0 40.7 jit_solution(11708769178853179268)
XLA Ops:
  0.6 0.0 copy-start.1
  0.6 0.8 %reshape.7 = s32[8,32]{1,0:T(8,128)S(1)} reshape(s32[8,2,16]{2,1,0:T(2,128)} %param.4) | data formatting | bytes 2048 | tf_op jit(solution)/shard_map/reshape | solution.py:503
  1.4 0.0 copy-done.1
  1.4 0.1 copy.5
  1.5 0.1 add_convert_fusion
  1.6 0.0 copy-start
  1.6 1.0 %copy-done = bf16[8,16,2048]{2,1,0:T(8,128)(2,1)S(1)} copy-done((bf16[8,16,2048]{2,1,0:T(8,128)(2,1)S(1)}, bf16[8,16,2048]{2,1,0:T(8,128)(2,1)}, u32[]{:S(2)}) %copy-start) | copy-done | bytes 524312
  2.6 36.7 %shard_map.50 = (f32[2,16,128]{2,1,0:T(8,128)S(1)}, f32[2,16,2048]{2,1,0:T(8,128)S(1)}) custom-call(bf16[8,16,2048]{2,1,0:T(8,128)(2,1)S(1)} %copy-done, f32[8,128]{1,0:T(8,128)S(1)} %pad.4.meta_ref), custom_call_target="tpu_custom_call" | custom-call | tf_op jit(solution)/shard_map/pallas_call | solution.py:509
  39.4 0.6 %copy.8 = f32[2,16,128]{2,1,0:T(8,128)} copy(f32[2,16,128]{2,1,0:T(8,128)S(1)} %get-tuple-element.4) | data formatting | bytes 32768
  40.0 0.7 %copy.9 = f32[2,16,2048]{2,1,0:T(8,128)} copy(f32[2,16,2048]{2,1,0:T(8,128)S(1)} %get-tuple-element.5) | data formatting | bytes 524288
  (1 shorter events, 0.0 us)
Async XLA Ops:
  0.6 0.8 %copy-start.1 = (s32[8,2]{0,1:T(2,128)S(1)}, s32[8,2]{0,1:T(2,128)}, u32[]{:S(2)}) copy-start(s32[8,2]{0,1:T(2,128)} %param.5) | copy-start | bytes 196
  1.6 1.0 %copy-start = (bf16[8,16,2048]{2,1,0:T(8,128)(2,1)S(1)}, bf16[8,16,2048]{2,1,0:T(8,128)(2,1)}, u32[]{:S(2)}) copy-start(bf16[8,16,2048]{2,1,0:T(8,128)(2,1)} %x_ref.1) | copy-start | bytes 1572868
